TPU v7x, 32 devices: a whole 2x2x4 slice. The times are simulated.
32 devices in a mesh: frame: 4 (over y, core), patch: 8 (over z, x).
Axes of the slice: x: 2, y: 2, z: 4, core: 2. Of those that a mesh axis runs over, the one named last changes fastest.
Arguments:
- q_space: bfloat16 [32, 8, 512, 128], P('frame', None, 'patch'), may hold values from -8 to 8
- k_space: bfloat16 [32, 8, 512, 128], P('frame', None, 'patch'), may hold values from -8 to 8
- v_space: bfloat16 [32, 8, 512, 128], P('frame', None, 'patch'), may hold values from -6 to 6
- d_out_space: bfloat16 [32, 8, 512, 128], P('frame', None, 'patch'), may hold values from -6 to 6
- q_time: bfloat16 [32, 8, 512, 128], P('frame', None, 'patch'), may hold values from -8 to 8
- k_time: bfloat16 [32, 8, 512, 128], P('frame', None, 'patch'), may hold values from -8 to 8
- v_time: bfloat16 [32, 8, 512, 128], P('frame', None, 'patch'), may hold values from -6 to 6
- d_out_time: bfloat16 [32, 8, 512, 128], P('frame', None, 'patch'), may hold values from -6 to 6
Outputs:
- grad_q_space: bfloat16 [32, 8, 512, 128], P('frame', None, 'patch')
- grad_k_space: bfloat16 [32, 8, 512, 128], P('frame', None, 'patch')
- grad_v_space: bfloat16 [32, 8, 512, 128], P('frame', None, 'patch')
- grad_q_time: bfloat16 [32, 8, 512, 128], P('frame', None, 'patch')
- grad_k_time: bfloat16 [32, 8, 512, 128], P('frame', None, 'patch')
- grad_v_time: bfloat16 [32, 8, 512, 128], P('frame', None, 'patch')
All inputs are finite; a program needn't handle non-finite values.
Results may differ from a plain program's by a relative error of at most 0.0071.
Values may be sent and summed in bfloat16 or wider, within the bound.
A program may use at most 128 MiB of HBM per device.

v0:
```python
import math

import jax
import jax.numpy as jnp
from jax import lax
from jax.sharding import PartitionSpec as P

SPACE_FORM = ("giqd", "gikd", "giqk")
TIME_FORM = ("qhpd", "khpd", "hpqk")


def contract(first_form, second_form, result_form, left, right):
    return jnp.einsum(
        first_form + "," + second_form + "->" + result_form,
        left,
        right,
        preferred_element_type=jnp.float32,
    )


def forward_pass(queries, key_rows, values, layout, causal):
    inverse_root_scale = 1.0 / math.sqrt(queries.shape[-1])
    score_logits = contract(layout[0], layout[1], layout[2], queries, key_rows) * inverse_root_scale
    if causal:
        length = score_logits.shape[-1]
        allowed = jnp.arange(length)[:, None] >= jnp.arange(length)[None, :]
        score_logits = jnp.where(allowed, score_logits, -1e30)
    row_max = jnp.max(score_logits, axis=-1, keepdims=True)
    raised = jnp.exp(score_logits - row_max)
    softmax_rows = raised / jnp.sum(raised, axis=-1, keepdims=True)
    weight_probabilities = softmax_rows.astype(jnp.bfloat16)
    output_tensor = contract(layout[2], layout[1], layout[0], weight_probabilities, values)
    return (softmax_rows, weight_probabilities, output_tensor)


def backward_pass(queries, key_rows, values, out_grad, state, layout):
    softmax_rows, weight_probabilities, output_tensor = state
    inverse_root_scale = 1.0 / math.sqrt(queries.shape[-1])
    delta_rows = jnp.einsum(
        layout[0] + "," + layout[0] + "->" + layout[2][:-1],
        out_grad.astype(jnp.float32),
        output_tensor,
    )
    value_gradient = contract(
        layout[2], layout[0], layout[1], weight_probabilities, out_grad
    ).astype(jnp.bfloat16)
    probability_gradient = contract(layout[0], layout[1], layout[2], out_grad, values)
    logit_gradient = (softmax_rows * (probability_gradient - delta_rows[..., None])).astype(
        jnp.bfloat16
    )
    query_gradient = (
        contract(layout[2], layout[1], layout[0], logit_gradient, key_rows) * inverse_root_scale
    ).astype(jnp.bfloat16)
    key_gradient = (
        contract(layout[2], layout[0], layout[1], logit_gradient, queries) * inverse_root_scale
    ).astype(jnp.bfloat16)
    return (query_gradient, key_gradient, value_gradient)


def attention_grads(queries, key_rows, values, out_grad, layout, causal):
    state = forward_pass(queries, key_rows, values, layout, causal)
    return backward_pass(queries, key_rows, values, out_grad, state, layout)


def space_items(parts):
    return attention_grads(parts[0], parts[1], parts[2], parts[3], SPACE_FORM, False)


def time_items(parts):
    return attention_grads(parts[0], parts[1], parts[2], parts[3], TIME_FORM, True)


def per_device(q_space, k_space, v_space, d_out_space, q_time, k_time, v_time, d_out_time):
    frame_dev, head_count, patch_dev, head_dim = q_space.shape
    patch_devices = lax.axis_size("patch")
    per_group = frame_dev * head_count // patch_devices

    def regroup(block):
        return block.reshape(patch_devices, per_group, patch_dev, head_dim)

    space_grads = space_items(
        (
            lax.all_to_all(regroup(q_space), "patch", split_axis=0, concat_axis=2, tiled=True),
            lax.all_to_all(regroup(k_space), "patch", split_axis=0, concat_axis=2, tiled=True),
            lax.all_to_all(regroup(v_space), "patch", split_axis=0, concat_axis=2, tiled=True),
            lax.all_to_all(regroup(d_out_space), "patch", split_axis=0, concat_axis=2, tiled=True),
        )
    )
    time_grads = time_items(
        (
            lax.all_to_all(q_time, "frame", split_axis=2, concat_axis=0, tiled=True),
            lax.all_to_all(k_time, "frame", split_axis=2, concat_axis=0, tiled=True),
            lax.all_to_all(v_time, "frame", split_axis=2, concat_axis=0, tiled=True),
            lax.all_to_all(d_out_time, "frame", split_axis=2, concat_axis=0, tiled=True),
        )
    )
    space_back = (
        lax.all_to_all(space_grads[0], "patch", split_axis=2, concat_axis=0, tiled=True),
        lax.all_to_all(space_grads[1], "patch", split_axis=2, concat_axis=0, tiled=True),
        lax.all_to_all(space_grads[2], "patch", split_axis=2, concat_axis=0, tiled=True),
    )
    time_back = (
        lax.all_to_all(time_grads[0], "frame", split_axis=0, concat_axis=2, tiled=True),
        lax.all_to_all(time_grads[1], "frame", split_axis=0, concat_axis=2, tiled=True),
        lax.all_to_all(time_grads[2], "frame", split_axis=0, concat_axis=2, tiled=True),
    )
    shape_dev = (frame_dev, head_count, patch_dev, head_dim)
    return (
        space_back[0].reshape(shape_dev),
        space_back[1].reshape(shape_dev),
        space_back[2].reshape(shape_dev),
        time_back[0],
        time_back[1],
        time_back[2],
    )


def solution(mesh):
    in_specs = (
        P("frame", None, "patch", None),
        P("frame", None, "patch", None),
        P("frame", None, "patch", None),
        P("frame", None, "patch", None),
        P("frame", None, "patch", None),
        P("frame", None, "patch", None),
        P("frame", None, "patch", None),
        P("frame", None, "patch", None),
    )
    out_specs = (
        P("frame", None, "patch", None),
        P("frame", None, "patch", None),
        P("frame", None, "patch", None),
        P("frame", None, "patch", None),
        P("frame", None, "patch", None),
        P("frame", None, "patch", None),
    )
    return jax.shard_map(
        per_device, mesh=mesh, in_specs=in_specs, out_specs=out_specs, check_vma=False
    )
```

profile of v0, /device:TPU:0, one launch (start us, length us, event | category | flops | bytes accessed | tf_op | source)
XLA Modules:
  0.0 347.8 jit_solution(8858422836417254673)
XLA Ops:
  3.6 4.2 %all-to-all-start.10 = ((bf16[8,8,64,128]{3,1,0,2:T(8,128)(2,1)}), bf16[8,8,64,128]{3,1,0,2:T(8,128)(2,1)S(1)}, u32[]{:S(2)}, u32[]{:S(2)}) async-start(bf16[8,8,64,128]{3,1,0,2:T(8,128)(2,1)} %copy.50), calls=%async_computation.10 | async-start | bytes 2097152 | tf_op jit(solution)/shard_map/all_to_all | solution.py:93
  9.5 12.8 %all-to-all-done.10 = bf16[8,8,64,128]{3,1,0,2:T(8,128)(2,1)S(1)} async-done(((bf16[8,8,64,128]{3,1,0,2:T(8,128)(2,1)}), bf16[8,8,64,128]{3,1,0,2:T(8,128)(2,1)S(1)}, u32[]{:S(2)}, u32[]{:S(2)}) %all-to-all-start.10) | async-done | bytes 1048608 | tf_op jit(solution)/shard_map/all_to_all | solution.py:93
  28.5 12.8 %all-to-all-done.8 = bf16[8,8,64,128]{3,1,0,2:T(8,128)(2,1)S(1)} async-done(((bf16[8,8,64,128]{3,1,0,2:T(8,128)(2,1)}), bf16[8,8,64,128]{3,1,0,2:T(8,128)(2,1)S(1)}, u32[]{:S(2)}, u32[]{:S(2)}) %all-to-all-start.8) | async-done | bytes 1048608 | tf_op jit(solution)/shard_map/all_to_all | solution.py:92
  46.4 12.8 %all-to-all-done.7 = bf16[8,8,64,128]{3,1,0,2:T(8,128)(2,1)S(1)} async-done(((bf16[8,8,64,128]{3,1,0,2:T(8,128)(2,1)}), bf16[8,8,64,128]{3,1,0,2:T(8,128)(2,1)S(1)}, u32[]{:S(2)}, u32[]{:S(2)}) %all-to-all-start.7) | async-done | bytes 1048608 | tf_op jit(solution)/shard_map/all_to_all | solution.py:91
  59.2 4.3 %all-to-all-start.9 = ((bf16[8,8,64,128]{3,1,0,2:T(8,128)(2,1)}), bf16[8,8,64,128]{3,1,0,2:T(8,128)(2,1)}, u32[]{:S(2)}, u32[]{:S(2)}) async-start(bf16[8,8,64,128]{3,1,0,2:T(8,128)(2,1)} %copy.48), calls=%async_computation.9 | async-start | bytes 2097152 | tf_op jit(solution)/shard_map/all_to_all | solution.py:94
  65.9 12.1 %all-to-all-done.9 = bf16[8,8,64,128]{3,1,0,2:T(8,128)(2,1)} async-done(((bf16[8,8,64,128]{3,1,0,2:T(8,128)(2,1)}), bf16[8,8,64,128]{3,1,0,2:T(8,128)(2,1)}, u32[]{:S(2)}, u32[]{:S(2)}) %all-to-all-start.9) | async-done | bytes 1048608 | tf_op jit(solution)/shard_map/all_to_all | solution.py:94
  84.0 17.7 %all_to_all.240 = bf16[32,8,16,128]{3,2,1,0:T(8,128)(2,1)} all-to-all(bf16[32,8,16,128]{3,2,1,0:T(8,128)(2,1)S(1)} %copy.54), channel_id=1, replica_groups=mesh['frame'=4,'patch'=8] {'frame'}, dimensions={0} | all-to-all | bytes 2097152 | tf_op jit(solution)/shard_map/all_to_all | solution.py:103
  101.8 32.0 %all_to_all.241 = bf16[8,8,64,128]{3,2,1,0:T(8,128)(2,1)} all-to-all(bf16[8,8,64,128]{3,2,1,0:T(8,128)(2,1)S(1)} %copy-done.11), channel_id=1, replica_groups=mesh['frame'=4,'patch'=8] {'patch'}, dimensions={0} | all-to-all | bytes 2097152 | tf_op jit(solution)/shard_map/all_to_all | solution.py:86
  133.8 28.8 %all_to_all.242 = bf16[8,8,64,128]{3,2,1,0:T(8,128)(2,1)} all-to-all(bf16[8,8,64,128]{3,2,1,0:T(8,128)(2,1)S(1)} %copy-done.12), channel_id=1, replica_groups=mesh['frame'=4,'patch'=8] {'patch'}, dimensions={0} | all-to-all | bytes 2097152 | tf_op jit(solution)/shard_map/all_to_all | solution.py:83
  162.5 28.8 %all_to_all.243 = bf16[8,8,64,128]{3,2,1,0:T(8,128)(2,1)} all-to-all(bf16[8,8,64,128]{3,2,1,0:T(8,128)(2,1)S(1)} %copy-done.13), channel_id=1, replica_groups=mesh['frame'=4,'patch'=8] {'patch'}, dimensions={0} | all-to-all | bytes 2097152 | tf_op jit(solution)/shard_map/all_to_all | solution.py:84
  191.3 4.2 %all-to-all-start.3 = ((bf16[8,8,64,128]{3,2,1,0:T(8,128)(2,1)}), bf16[8,8,64,128]{3,2,1,0:T(8,128)(2,1)}, u32[]{:S(2)}, u32[]{:S(2)}) async-start(bf16[8,8,64,128]{3,2,1,0:T(8,128)(2,1)} %param.10), calls=%async_computation.3 | async-start | bytes 2097152 | tf_op jit(solution)/shard_map/all_to_all | solution.py:85
  201.1 5.0 %fusion.54 = (f32[8,512]{1,0:T(8,128)S(1)}, f32[8,512,512]{1,2,0:T(8,128)}) fusion(bf16[8,512,128]{2,1,0:T(8,128)(2,1)S(1)} %bitcast.141, bf16[8,512,128]{2,1,0:T(8,128)(2,1)S(1)} %bitcast.139), kind=kOutput, calls=%fused_computation.57 | convolution fusion | flops 543162880 | bytes 10502144 | tf_op jit(solution)/shard_map/sub | solution.py:29
  206.1 14.4 %all-to-all-done.3 = bf16[8,8,64,128]{3,2,1,0:T(8,128)(2,1)} async-done(((bf16[8,8,64,128]{3,2,1,0:T(8,128)(2,1)}), bf16[8,8,64,128]{3,2,1,0:T(8,128)(2,1)}, u32[]{:S(2)}, u32[]{:S(2)}) %all-to-all-start.3) | async-done | bytes 1048608 | tf_op jit(solution)/shard_map/all_to_all | solution.py:85
  224.2 4.7 %fusion.6 = bf16[8,512,512]{1,2,0:T(8,128)(2,1)S(1)} fusion(f32[8,512,512]{1,2,0:T(8,128)} %get-tuple-element.7, f32[8,512]{1,0:T(8,128)S(1)} %get-tuple-element.6), kind=kLoop, calls=%fused_computation.8 | loop fusion | flops 4194304 | bytes 12599296 | tf_op jit(solution)/shard_map/convert_element_type | solution.py:31
  233.9 4.6 %all-to-all-done.12 = bf16[32,8,16,128]{3,2,1,0:T(8,128)(2,1)S(1)} async-done(((bf16[32,8,16,128]{3,2,1,0:T(8,128)(2,1)}), bf16[32,8,16,128]{3,2,1,0:T(8,128)(2,1)S(1)}, u32[]{:S(2)}, u32[]{:S(2)}) %all-to-all-start.12) | async-done | bytes 1048608 | tf_op jit(solution)/shard_map/all_to_all | solution.py:104
  242.0 5.3 %multiply_convert_fusion = bf16[8,512,512]{1,2,0:T(8,128)(2,1)S(1)} fusion(f32[8,512]{1,0:T(8,128)S(1)} %multiply_reduce_fusion.2, f32[8,512,512]{1,2,0:T(8,128)} %get-tuple-element.7, f32[8,512]{1,0:T(8,128)S(1)} %get-tuple-element.6, bf16[8,512,128]{2,1,0:T(8,128)(2,1)} %bitcast.146, bf16[8,512,128]{2,1,0:T(8,128)(2,1)} %bitcast.154), kind=kOutput, calls=%fused_computation.2 | convolution fusion | flops 545259520 | bytes 14712832 | tf_op jit(solution)/shard_map/giqd,gikd->giqk/dot_general | solution.py:13
  250.9 5.5 %all-to-all-done.13 = bf16[32,8,16,128]{3,2,1,0:T(8,128)(2,1)S(1)} async-done(((bf16[32,8,16,128]{3,2,1,0:T(8,128)(2,1)}), bf16[32,8,16,128]{3,2,1,0:T(8,128)(2,1)S(1)}, u32[]{:S(2)}, u32[]{:S(2)}) %all-to-all-start.13) | async-done | bytes 1048608 | tf_op jit(solution)/shard_map/all_to_all | solution.py:105
  260.0 3.7 %fusion.11 = bf16[1,8,512,128]{3,2,1,0:T(8,128)(2,1)S(1)} fusion(bf16[8,512,512]{1,2,0:T(8,128)(2,1)} %copy-done, bf16[8,512,128]{2,1,0:T(8,128)(2,1)} %bitcast.142), kind=kOutput, calls=%fused_computation.24 | convolution fusion | flops 537919488 | bytes 6291456 | tf_op jit(solution)/shard_map/giqk,giqd->gikd/dot_general | solution.py:13
  265.4 20.4 %all-to-all-done.4 = bf16[1,8,512,128]{3,1,0,2:T(8,128)(2,1)S(1)} async-done(((bf16[1,8,512,128]{3,1,0,2:T(8,128)(2,1)}), bf16[1,8,512,128]{3,1,0,2:T(8,128)(2,1)S(1)}, u32[]{:S(2)}, u32[]{:S(2)}) %all-to-all-start.4) | async-done | bytes 1048608 | tf_op jit(solution)/shard_map/all_to_all | solution.py:98
  285.7 4.2 %all-to-all-start.5 = ((bf16[1,8,512,128]{3,1,0,2:T(8,128)(2,1)}), bf16[1,8,512,128]{3,1,0,2:T(8,128)(2,1)}, u32[]{:S(2)}, u32[]{:S(2)}) async-start(bf16[1,8,512,128]{3,1,0,2:T(8,128)(2,1)} %copy.40), calls=%async_computation.5 | async-start | bytes 2097152 | tf_op jit(solution)/shard_map/all_to_all | solution.py:99
  290.0 3.7 %fusion.8 = bf16[1,8,512,128]{3,2,1,0:T(8,128)(2,1)S(1)} fusion(bf16[8,512,512]{1,2,0:T(8,128)(2,1)} %copy-done.1, bf16[8,512,128]{2,1,0:T(8,128)(2,1)} %bitcast.147), kind=kOutput, calls=%fused_computation.21 | convolution fusion | flops 537395200 | bytes 6291456 | tf_op jit(solution)/shard_map/giqk,giqd->gikd/dot_general | solution.py:13
  295.4 20.2 %all-to-all-done.5 = bf16[1,8,512,128]{3,1,0,2:T(8,128)(2,1)} async-done(((bf16[1,8,512,128]{3,1,0,2:T(8,128)(2,1)}), bf16[1,8,512,128]{3,1,0,2:T(8,128)(2,1)}, u32[]{:S(2)}, u32[]{:S(2)}) %all-to-all-start.5) | async-done | bytes 1048608 | tf_op jit(solution)/shard_map/all_to_all | solution.py:99
  315.6 4.2 %all-to-all-start.6 = ((bf16[1,8,512,128]{3,1,0,2:T(8,128)(2,1)}), bf16[1,8,512,128]{3,1,0,2:T(8,128)(2,1)}, u32[]{:S(2)}, u32[]{:S(2)}) async-start(bf16[1,8,512,128]{3,1,0,2:T(8,128)(2,1)} %copy.42), calls=%async_computation.6 | async-start | bytes 2097152 | tf_op jit(solution)/shard_map/all_to_all | solution.py:100
  327.4 17.9 %all-to-all-done.6 = bf16[1,8,512,128]{3,1,0,2:T(8,128)(2,1)} async-done(((bf16[1,8,512,128]{3,1,0,2:T(8,128)(2,1)}), bf16[1,8,512,128]{3,1,0,2:T(8,128)(2,1)}, u32[]{:S(2)}, u32[]{:S(2)}) %all-to-all-start.6) | async-done | bytes 1048608 | tf_op jit(solution)/shard_map/all_to_all | solution.py:100
  (78 shorter events, 62.4 us)
Async XLA Ops:
  0.6 7.2 %copy-start.8 = (bf16[8,8,64,128]{3,2,1,0:T(8,128)(2,1)S(1)}, bf16[8,8,64,128]{3,2,1,0:T(8,128)(2,1)}, u32[]{:S(2)}) copy-start(bf16[8,8,64,128]{3,2,1,0:T(8,128)(2,1)} %param.13) | copy-start | bytes 3145732
  3.6 18.7 %all-to-all-start.10 = ((bf16[8,8,64,128]{3,1,0,2:T(8,128)(2,1)}), bf16[8,8,64,128]{3,1,0,2:T(8,128)(2,1)S(1)}, u32[]{:S(2)}, u32[]{:S(2)}) async-start(bf16[8,8,64,128]{3,1,0,2:T(8,128)(2,1)} %copy.50), calls=%async_computation.10 | async-start | bytes 2097152 | tf_op jit(solution)/shard_map/all_to_all | solution.py:93
  7.8 19.0 %copy-start.9 = (bf16[8,8,64,128]{3,2,1,0:T(8,128)(2,1)S(1)}, bf16[8,8,64,128]{3,2,1,0:T(8,128)(2,1)}, u32[]{:S(2)}) copy-start(bf16[8,8,64,128]{3,2,1,0:T(8,128)(2,1)} %param.12) | copy-start | bytes 3145732
  23.3 18.0 %all-to-all-start.8 = ((bf16[8,8,64,128]{3,1,0,2:T(8,128)(2,1)}), bf16[8,8,64,128]{3,1,0,2:T(8,128)(2,1)S(1)}, u32[]{:S(2)}, u32[]{:S(2)}) async-start(bf16[8,8,64,128]{3,1,0,2:T(8,128)(2,1)} %copy.46), calls=%async_computation.8 | async-start | bytes 2097152 | tf_op jit(solution)/shard_map/all_to_all | solution.py:92
  28.5 16.3 %copy-start.10 = (bf16[8,8,64,128]{3,2,1,0:T(8,128)(2,1)S(1)}, bf16[8,8,64,128]{3,2,1,0:T(8,128)(2,1)}, u32[]{:S(2)}) copy-start(bf16[8,8,64,128]{3,2,1,0:T(8,128)(2,1)} %param.15) | copy-start | bytes 3145732
  41.2 18.0 %all-to-all-start.7 = ((bf16[8,8,64,128]{3,1,0,2:T(8,128)(2,1)}), bf16[8,8,64,128]{3,1,0,2:T(8,128)(2,1)S(1)}, u32[]{:S(2)}, u32[]{:S(2)}) async-start(bf16[8,8,64,128]{3,1,0,2:T(8,128)(2,1)} %copy.44), calls=%async_computation.7 | async-start | bytes 2097152 | tf_op jit(solution)/shard_map/all_to_all | solution.py:91
  59.2 18.8 %all-to-all-start.9 = ((bf16[8,8,64,128]{3,1,0,2:T(8,128)(2,1)}), bf16[8,8,64,128]{3,1,0,2:T(8,128)(2,1)}, u32[]{:S(2)}, u32[]{:S(2)}) async-start(bf16[8,8,64,128]{3,1,0,2:T(8,128)(2,1)} %copy.48), calls=%async_computation.9 | async-start | bytes 2097152 | tf_op jit(solution)/shard_map/all_to_all | solution.py:94
  63.5 14.5 %copy-start.16 = (bf16[8,8,64,128]{3,1,0,2:T(8,128)(2,1)S(1)}, bf16[8,8,64,128]{3,1,0,2:T(8,128)(2,1)}, u32[]{:S(2)}) copy-start(bf16[8,8,64,128]{3,1,0,2:T(8,128)(2,1)} %copy-done.15) | copy-start | bytes 3145732
  78.0 3.1 copy-start.17
  78.0 3.1 copy-start.20
  83.6 18.2 %copy-start.11 = (bf16[8,8,64,128]{3,2,1,0:T(8,128)(2,1)S(1)}, bf16[8,8,64,128]{3,2,1,0:T(8,128)(2,1)}, u32[]{:S(2)}) copy-start(bf16[8,8,64,128]{3,2,1,0:T(8,128)(2,1)} %param.11) | copy-start | bytes 3145732
  84.0 49.7 %copy-start.12 = (bf16[8,8,64,128]{3,2,1,0:T(8,128)(2,1)S(1)}, bf16[8,8,64,128]{3,2,1,0:T(8,128)(2,1)}, u32[]{:S(2)}) copy-start(bf16[8,8,64,128]{3,2,1,0:T(8,128)(2,1)} %param.8) | copy-start | bytes 3145732
  101.8 60.7 %copy-start.13 = (bf16[8,8,64,128]{3,2,1,0:T(8,128)(2,1)S(1)}, bf16[8,8,64,128]{3,2,1,0:T(8,128)(2,1)}, u32[]{:S(2)}) copy-start(bf16[8,8,64,128]{3,2,1,0:T(8,128)(2,1)} %param.9) | copy-start | bytes 3145732
  191.3 29.2 %all-to-all-start.3 = ((bf16[8,8,64,128]{3,2,1,0:T(8,128)(2,1)}), bf16[8,8,64,128]{3,2,1,0:T(8,128)(2,1)}, u32[]{:S(2)}, u32[]{:S(2)}) async-start(bf16[8,8,64,128]{3,2,1,0:T(8,128)(2,1)} %param.10), calls=%async_computation.3 | async-start | bytes 2097152 | tf_op jit(solution)/shard_map/all_to_all | solution.py:85
  200.6 5.5 %copy-start.14 = (bf16[1,8,8,64,128]{4,3,2,1,0:T(8,128)(2,1)}, bf16[1,8,8,64,128]{4,3,2,1,0:T(8,128)(2,1)S(1)}, u32[]{:S(2)}) copy-start(bf16[1,8,8,64,128]{4,3,2,1,0:T(8,128)(2,1)S(1)} %copy.32) | copy-start | bytes 3145732
  220.5 18.0 %all-to-all-start.12 = ((bf16[32,8,16,128]{3,2,1,0:T(8,128)(2,1)}), bf16[32,8,16,128]{3,2,1,0:T(8,128)(2,1)S(1)}, u32[]{:S(2)}, u32[]{:S(2)}) async-start(bf16[32,8,16,128]{3,2,1,0:T(8,128)(2,1)} %copy.56), calls=%async_computation.12 | async-start | bytes 2097152 | tf_op jit(solution)/shard_map/all_to_all | solution.py:104
  224.2 4.7 %copy-start.5 = (bf16[8,8,64,128]{3,2,1,0:T(8,128)(2,1)S(1)}, bf16[8,8,64,128]{3,2,1,0:T(8,128)(2,1)}, u32[]{:S(2)}) copy-start(bf16[8,8,64,128]{3,2,1,0:T(8,128)(2,1)} %all_to_all.241) | copy-start | bytes 3145732
  229.0 4.9 %copy-start.18 = (bf16[1,8,8,64,128]{4,3,2,1,0:T(8,128)(2,1)}, bf16[1,8,8,64,128]{4,3,2,1,0:T(8,128)(2,1)S(1)}, u32[]{:S(2)}) copy-start(bf16[1,8,8,64,128]{4,3,2,1,0:T(8,128)(2,1)S(1)} %copy.34) | copy-start | bytes 3145732
  238.4 18.0 %all-to-all-start.13 = ((bf16[32,8,16,128]{3,2,1,0:T(8,128)(2,1)}), bf16[32,8,16,128]{3,2,1,0:T(8,128)(2,1)S(1)}, u32[]{:S(2)}, u32[]{:S(2)}) async-start(bf16[32,8,16,128]{3,2,1,0:T(8,128)(2,1)} %copy.58), calls=%async_computation.13 | async-start | bytes 2097152 | tf_op jit(solution)/shard_map/all_to_all | solution.py:105
  256.4 29.3 %all-to-all-start.4 = ((bf16[1,8,512,128]{3,1,0,2:T(8,128)(2,1)}), bf16[1,8,512,128]{3,1,0,2:T(8,128)(2,1)S(1)}, u32[]{:S(2)}, u32[]{:S(2)}) async-start(bf16[1,8,512,128]{3,1,0,2:T(8,128)(2,1)} %copy.38), calls=%async_computation.4 | async-start | bytes 2097152 | tf_op jit(solution)/shard_map/all_to_all | solution.py:98
  285.7 4.3 %copy-start.3 = (bf16[1,8,512,128]{3,1,0,2:T(8,128)(2,1)}, bf16[1,8,512,128]{3,1,0,2:T(8,128)(2,1)S(1)}, u32[]{:S(2)}) copy-start(bf16[1,8,512,128]{3,1,0,2:T(8,128)(2,1)S(1)} %all-to-all-done.4) | copy-start | bytes 3145732
  285.7 29.9 %all-to-all-start.5 = ((bf16[1,8,512,128]{3,1,0,2:T(8,128)(2,1)}), bf16[1,8,512,128]{3,1,0,2:T(8,128)(2,1)}, u32[]{:S(2)}, u32[]{:S(2)}) async-start(bf16[1,8,512,128]{3,1,0,2:T(8,128)(2,1)} %copy.40), calls=%async_computation.5 | async-start | bytes 2097152 | tf_op jit(solution)/shard_map/all_to_all | solution.py:99
  293.7 26.1 %copy-start.2 = (bf16[32,8,16,128]{3,2,1,0:T(8,128)(2,1)S(1)}, bf16[32,8,16,128]{3,2,1,0:T(8,128)(2,1)}, u32[]{:S(2)}) copy-start(bf16[32,8,16,128]{3,2,1,0:T(8,128)(2,1)} %all_to_all.240) | copy-start | bytes 3145732
  315.6 29.7 %all-to-all-start.6 = ((bf16[1,8,512,128]{3,1,0,2:T(8,128)(2,1)}), bf16[1,8,512,128]{3,1,0,2:T(8,128)(2,1)}, u32[]{:S(2)}, u32[]{:S(2)}) async-start(bf16[1,8,512,128]{3,1,0,2:T(8,128)(2,1)} %copy.42), calls=%async_computation.6 | async-start | bytes 2097152 | tf_op jit(solution)/shard_map/all_to_all | solution.py:100
  (8 other events, 13.8 us)
where the time goes:
time: 349 us; the launch traced here: 348 us
  waiting for transfers between devices  133 us (38%)
  blocking collectives  107 us (31%)
  starting transfers between devices  39 us (11%)
  local copies, waits for them, and re-layouts  31.2 us (9%)
  matrix products  31.2 us (9%)
  other arithmetic  4.69 us (1%)
    all_to_all x1, blocking collectives, per_device(): lax.all_to_all(regroup(d_out_space), 'patch', split_axis=0, concat_axis=2...  32 us
    all_to_all x1, blocking collectives, per_device(): lax.all_to_all(regroup(q_space), 'patch', split_axis=0, concat_axis=2, ti...  28.8 us
    all_to_all x1, blocking collectives, per_device(): lax.all_to_all(regroup(k_space), 'patch', split_axis=0, concat_axis=2, ti...  28.8 us
    dot_general x10, matrix products, contract(): jnp.einsum(first_form + ',' + second_form + '->' + result_form, left, rig...  23.8 us
    all_to_all x1, waiting for transfers between devices, per_device(): lax.all_to_all(space_grads[0], 'patch', split_axis=2, concat_axis=0, tile...  20.4 us
    all_to_all x1, waiting for transfers between devices, per_device(): lax.all_to_all(space_grads[1], 'patch', split_axis=2, concat_axis=0, tile...  20.2 us
    all_to_all x1, waiting for transfers between devices, per_device(): lax.all_to_all(space_grads[2], 'patch', split_axis=2, concat_axis=0, tile...  17.9 us
    all_to_all x1, blocking collectives, per_device(): lax.all_to_all(time_grads[0], 'frame', split_axis=0, concat_axis=2, tiled...  17.7 us
  transfers between devices with their start and end apart: 10, of which 10 were waited for; matrix products, arithmetic and copies ran while one was open for 15% of the time, Pallas kernels for 0%

commit v1 on v0

v1 whole, which is shorter than its diff:
```python
import functools
import math

import jax
import jax.numpy as jnp
from jax import lax
from jax.experimental import pallas as pl
from jax.experimental.pallas import tpu as pltpu
from jax.sharding import PartitionSpec as P

MESH = pl.DeviceIdType.MESH
ROWS = 16
BLOCK = 256


def flip_dot(left, right):
    return lax.dot_general(
        left, right, (((1,), (1,)), ((), ())), preferred_element_type=jnp.float32
    )


def lead_dot(left, right):
    return lax.dot_general(
        left, right, (((0,), (0,)), ((), ())), preferred_element_type=jnp.float32
    )


def attend(length, scale, group, load, store, dk_acc, dv_acc):
    for start in range(0, length, BLOCK):
        rows = min(BLOCK, length - start)
        seen = start + rows if group else length
        query = load(0, start, rows)
        keys = load(1, 0, seen)
        values = load(2, 0, seen)
        upstream = load(3, start, rows)
        scores = flip_dot(keys, query) * scale
        if group:
            gap = (
                lax.broadcasted_iota(jnp.int32, (seen, rows), 1)
                + start
                - lax.broadcasted_iota(jnp.int32, (seen, rows), 0)
            )
            allowed = jnp.logical_and(gap >= 0, (gap & (group - 1)) == 0)
            scores = jnp.where(allowed, scores, -1e30)
        raised = jnp.exp(scores - jnp.max(scores, axis=0, keepdims=True))
        soft = raised * (1.0 / jnp.sum(raised, axis=0, keepdims=True))
        weights = soft.astype(jnp.bfloat16)
        grad_prob = flip_dot(values, upstream)
        delta = jnp.sum(weights.astype(jnp.float32) * grad_prob, axis=0, keepdims=True)
        grad_score = (soft * (grad_prob - delta)).astype(jnp.bfloat16)
        dv = jnp.dot(weights, upstream, preferred_element_type=jnp.float32)
        dk = jnp.dot(grad_score, query, preferred_element_type=jnp.float32)
        store(0, start, (lead_dot(grad_score, keys) * scale).astype(jnp.bfloat16))
        if start == 0 and seen < length:
            dk_acc[pl.ds(seen, length - seen), :] = jnp.zeros((length - seen, dk.shape[1]), jnp.float32)
            dv_acc[pl.ds(seen, length - seen), :] = jnp.zeros((length - seen, dv.shape[1]), jnp.float32)
        if start == 0:
            dk_acc[pl.ds(0, seen), :] = dk
            dv_acc[pl.ds(0, seen), :] = dv
        else:
            dk_acc[pl.ds(0, seen), :] += dk
            dv_acc[pl.ds(0, seen), :] += dv
    store(1, 0, (dk_acc[pl.ds(0, length), :] * scale).astype(jnp.bfloat16))
    store(2, 0, dv_acc[pl.ds(0, length), :].astype(jnp.bfloat16))


def kernel(plan, *refs):
    space_in, time_in = refs[0:4], refs[4:8]
    space_out, time_out = refs[8:11], refs[11:14]
    (sp, sp_res, tm, tm_res, dk_acc, dv_acc) = refs[14:20]
    (sp_recv, sp_send, spb_recv, spb_send, tm_recv, tm_send, tmb_recv, tmb_send) = refs[20:]
    n_patch, n_frame, per_dev, rows, frames, heads_dev, span, scale = plan
    length = n_patch * rows
    me_p = lax.axis_index("patch")
    me_f = lax.axis_index("frame")

    def patch_peer(step):
        return lax.rem(me_p + step, n_patch)

    def frame_peer(step):
        return lax.rem(me_f + step, n_frame)

    def time_slot(owner):
        if span == rows:
            return pl.ds(owner * heads_dev, heads_dev), pl.ds(0, span)
        cuts = rows // span
        return (
            pl.ds(owner // cuts, 1),
            pl.ds(pl.multiple_of(lax.rem(owner, cuts) * span, span), span),
        )

    barrier = pltpu.get_barrier_semaphore()
    for step in range(1, n_patch):
        pl.semaphore_signal(barrier, inc=1, device_id={"patch": patch_peer(step)}, device_id_type=MESH)
    for step in range(1, n_frame):
        pl.semaphore_signal(barrier, inc=1, device_id={"frame": frame_peer(step)}, device_id_type=MESH)
    pl.semaphore_wait(barrier, n_patch + n_frame - 2)

    my_rows = pl.ds(pl.multiple_of(me_p * rows, rows), rows)
    pieces = max(1, per_dev // 2)
    piece_frames = frames // pieces

    def send_space(c):
        for step in range(1, n_patch):
            peer = patch_peer(step)
            for a in range(4):
                pltpu.make_async_remote_copy(
                    src_ref=space_in[a].at[peer * per_dev + c],
                    dst_ref=sp.at[c, a, my_rows],
                    send_sem=sp_send.at[c],
                    recv_sem=sp_recv.at[c],
                    device_id={"patch": peer},
                    device_id_type=MESH,
                ).start()
        for a in range(4):
            pltpu.make_async_copy(
                space_in[a].at[me_p * per_dev + c], sp.at[c, a, my_rows], sp_recv.at[c]
            ).start()

    def send_time(c):
        here = pl.ds(c * piece_frames, piece_frames)
        there = pl.ds(me_f * frames + c * piece_frames, piece_frames)
        for step in range(1, n_frame):
            peer = frame_peer(step)
            hs, ps = time_slot(peer)
            for a in range(4):
                pltpu.make_async_remote_copy(
                    src_ref=time_in[a].at[here, hs, ps],
                    dst_ref=tm.at[a, there],
                    send_sem=tm_send.at[0],
                    recv_sem=tm_recv.at[0],
                    device_id={"frame": peer},
                    device_id_type=MESH,
                ).start()
        hs, ps = time_slot(me_f)
        for a in range(4):
            pltpu.make_async_copy(time_in[a].at[here, hs, ps], tm.at[a, there], tm_recv.at[0]).start()

    @pl.loop(0, pieces)
    def _(c):
        send_space(c)
        send_time(c)

    @pl.loop(pieces, per_dev)
    def _(c):
        send_space(c)

    def all_time():
        pltpu.make_async_copy(tm, tm, tm_recv.at[0]).wait()
        units = span // ROWS
        total = n_frame * frames

        @pl.loop(0, heads_dev * units)
        def _(u):
            hh = u // units
            ps = pl.ds(pl.multiple_of(lax.rem(u, units) * ROWS, ROWS), ROWS)

            def load(a, start, count):
                block = tm[a, pl.ds(start // ROWS, count // ROWS), hh, ps, :]
                return block.reshape(count, block.shape[-1])

            def store(a, start, value):
                count = value.shape[0]
                tm_res[a, pl.ds(start // ROWS, count // ROWS), hh, ps, :] = value.reshape(
                    count // ROWS, ROWS, value.shape[1]
                )

            attend(total * ROWS, scale, ROWS, load, store, dk_acc, dv_acc)

        hs, ps = time_slot(me_f)
        for step in range(1, n_frame):
            peer = frame_peer(step)
            for a in range(3):
                pltpu.make_async_remote_copy(
                    src_ref=tm_res.at[a, pl.ds(peer * frames, frames)],
                    dst_ref=time_out[a].at[:, hs, ps],
                    send_sem=tmb_send.at[0],
                    recv_sem=tmb_recv.at[a],
                    device_id={"frame": peer},
                    device_id_type=MESH,
                ).start()
        for a in range(3):
            pltpu.make_async_copy(
                tm_res.at[a, pl.ds(me_f * frames, frames)], time_out[a].at[:, hs, ps], tmb_recv.at[a]
            ).start()

    @pl.loop(0, per_dev)
    def _(c):
        @pl.when(c == pieces)
        def _():
            all_time()

        pltpu.make_async_copy(sp.at[c], sp.at[c], sp_recv.at[c]).wait()

        def load(a, start, count):
            return sp[c, a, pl.ds(start, count), :]

        def store(a, start, value):
            sp_res[c, a, pl.ds(start, value.shape[0]), :] = value

        attend(length, scale, 0, load, store, dk_acc, dv_acc)
        seq = me_p * per_dev + c
        for step in range(1, n_patch):
            peer = patch_peer(step)
            for a in range(3):
                pltpu.make_async_remote_copy(
                    src_ref=sp_res.at[c, a, pl.ds(pl.multiple_of(peer * rows, rows), rows)],
                    dst_ref=space_out[a].at[seq],
                    send_sem=spb_send.at[c],
                    recv_sem=spb_recv.at[a],
                    device_id={"patch": peer},
                    device_id_type=MESH,
                ).start()
        for a in range(3):
            pltpu.make_async_copy(sp_res.at[c, a, my_rows], space_out[a].at[seq], spb_recv.at[a]).start()

    others = pl.ds(0, length - rows)
    away = pl.ds(0, (n_frame - 1) * frames)

    @pl.loop(0, per_dev)
    def _(c):
        pltpu.make_async_copy(sp.at[c, :, others], sp.at[c, :, others], sp_send.at[c]).wait()
        pltpu.make_async_copy(sp_res.at[c, :, others], sp_res.at[c, :, others], spb_send.at[c]).wait()

    pltpu.make_async_copy(tm.at[:, away], tm.at[:, away], tm_send.at[0]).wait()
    pltpu.make_async_copy(tm_res.at[:, away], tm_res.at[:, away], tmb_send.at[0]).wait()
    for a in range(3):
        pltpu.make_async_copy(time_out[a], time_out[a], tmb_recv.at[a]).wait()
        pltpu.make_async_copy(space_out[a], space_out[a], spb_recv.at[a]).wait()


def per_device(n_frame, n_patch, *blocks):
    frames, heads, rows, dim = blocks[0].shape
    per_dev = frames * heads // n_patch
    if n_frame <= heads:
        heads_dev, span = heads // n_frame, rows
    else:
        heads_dev, span = 1, rows * heads // n_frame
    length = n_patch * rows
    total = n_frame * frames
    scale = 1.0 / math.sqrt(dim)
    plan = (n_patch, n_frame, per_dev, rows, frames, heads_dev, span, scale)
    longest = max(length, total * ROWS)
    flat = (frames * heads, rows, dim)
    whole = (frames, heads, rows, dim)
    bf16 = jnp.bfloat16
    hbm = pl.BlockSpec(memory_space=pl.ANY)
    dma = pltpu.SemaphoreType.DMA
    outs = pl.pallas_call(
        functools.partial(kernel, plan),
        out_shape=[jax.ShapeDtypeStruct(flat, bf16)] * 3 + [jax.ShapeDtypeStruct(whole, bf16)] * 3,
        in_specs=[hbm] * 8,
        out_specs=[hbm] * 6,
        scratch_shapes=[
            pltpu.VMEM((per_dev, 4, length, dim), bf16),
            pltpu.VMEM((per_dev, 3, length, dim), bf16),
            pltpu.VMEM((4, total, heads_dev, span, dim), bf16),
            pltpu.VMEM((3, total, heads_dev, span, dim), bf16),
            pltpu.VMEM((longest, dim), jnp.float32),
            pltpu.VMEM((longest, dim), jnp.float32),
            dma((per_dev,)),
            dma((per_dev,)),
            dma((3,)),
            dma((per_dev,)),
            dma((1,)),
            dma((1,)),
            dma((3,)),
            dma((1,)),
        ],
        compiler_params=pltpu.CompilerParams(
            collective_id=0, has_side_effects=True, vmem_limit_bytes=56 * 1024 * 1024
        ),
    )(*[b.reshape(flat) for b in blocks[:4]], *blocks[4:])
    return tuple(o.reshape(whole) for o in outs)


def solution(mesh):
    spec = P("frame", None, "patch", None)
    return jax.shard_map(
        functools.partial(per_device, mesh.shape["frame"], mesh.shape["patch"]),
        mesh=mesh,
        in_specs=(spec,) * 8,
        out_specs=(spec,) * 6,
        check_vma=False,
    )
```

time: 349 us -> 174 us (0.50)
  Pallas kernels: 0 us -> 163 us
  waiting for transfers between devices: 133 us -> 0 us
  blocking collectives: 107 us -> 0 us
  starting transfers between devices: 39 us -> 0 us
  matrix products: 31.2 us -> 0 us
  local copies, waits for them, and re-layouts: 31.2 us -> 9.73 us
  other arithmetic: 4.69 us -> 0 us
    pallas_call x0 -> x1, Pallas kernels: none -> 163 us  [per_device(): pl.pallas_call(functools.partial(kernel, plan), out_shape=[jax.ShapeDtype...]
    all_to_all x10 -> x0, waiting for transfers between devices: 133 us -> none  [the longest x1 20.4 us: per_device(): lax.all_to_all(space_grads[0], 'patch', split_axis=2, concat_axis=0, tile...]
    all_to_all x4 -> x0, blocking collectives: 107 us -> none  [the longest x1 32 us: per_device(): lax.all_to_all(regroup(d_out_space), 'patch', split_axis=0, concat_axis=2...]
    all_to_all x10 -> x0, starting transfers between devices: 39 us -> none  [the longest x1 4.25 us: per_device(): lax.all_to_all(d_out_time, 'frame', split_axis=2, concat_axis=0, tiled=True)]
    dot_general x10 -> x0, matrix products: 23.8 us -> none  [contract(): jnp.einsum(first_form + ',' + second_form + '->' + result_form, left, rig...]
    all_to_all x10 -> x0, local copies, waits for them, and re-layouts: 12.3 us -> none  [the longest x1 2.48 us: per_device(): lax.all_to_all(space_grads[2], 'patch', split_axis=2, concat_axis=0, tile...]
    convert_element_type x6 -> x0, local copies, waits for them, and re-layouts: 8.12 us -> none  [the longest x2 3.04 us: backward_pass(): value_gradient = contract(layout[2], layout[0], layout[1], weight_probabi...]
    sub x2 -> x0, matrix products: 7.39 us -> none  [forward_pass(): raised = jnp.exp(score_logits - row_max)]
  transfers between devices with their start and end apart: 10 -> 0, of which waited for: 10 -> 0; matrix products, arithmetic and copies ran while one was open for 15% -> 0% of each run, Pallas kernels for 0% -> 0%
where the time goes in v1:
time: 174 us
  Pallas kernels  163 us (94%)
  local copies, waits for them, and re-layouts  9.73 us (6%)
    pallas_call x1, Pallas kernels, per_device(): pl.pallas_call(functools.partial(kernel, plan), out_shape=[jax.ShapeDtype...  163 us
    unnamed x16, local copies, waits for them, and re-layouts  9.73 us

profile of v1, /device:TPU:0, one launch (start us, length us, event | category | flops | bytes accessed | tf_op | source)
XLA Modules:
  0.0 173.5 jit_solution(4137285313456955808)
XLA Ops:
  0.6 163.1 %shard_map.127 = (bf16[64,64,128]{2,1,0:T(8,128)(2,1)}, bf16[64,64,128]{2,1,0:T(8,128)(2,1)}, bf16[64,64,128]{2,1,0:T(8,128)(2,1)}, bf16[8,8,64,128]{3,2,1,0:T(8...) custom-call(bf16[64,64,128]{2,1,0:T(8,128)(2,1)} %bitcast.10, ...), custom_call_target="tpu_custom_call" | custom-call | tf_op jit(solution)/shard_map/pallas_call | solution.py:249
  163.8 0.0 copy-start.4
  163.8 2.4 %copy.20 = bf16[8,8,64,128]{3,2,1,0:T(8,128)(2,1)} copy(bf16[8,8,64,128]{3,2,1,0:T(8,128)(2,1)} %bitcast.9) | data formatting | bytes 2097152
  166.1 0.0 copy-done.4
  166.1 0.0 copy-start.3
  166.1 1.0 copy.21
  167.1 0.6 copy-done.3
  167.7 0.0 copy-start.2
  167.7 1.0 copy.22
  168.7 0.6 copy-done.2
  169.3 0.0 copy-start.1
  169.3 1.0 copy.23
  170.3 0.6 copy-done.1
  170.9 0.0 copy-start
  171.0 1.0 copy.24
  171.9 0.6 copy-done
  172.6 1.0 copy.25
Async XLA Ops:
  163.8 2.4 %copy-start.4 = (bf16[64,64,128]{2,1,0:T(8,128)(2,1)S(1)}, bf16[64,64,128]{2,1,0:T(8,128)(2,1)}, u32[]{:S(2)}) copy-start(bf16[64,64,128]{2,1,0:T(8,128)(2,1)} %get-tuple-element.13) | copy-start | bytes 3145732
  166.1 1.6 copy-start.3
  167.7 1.6 copy-start.2
  169.3 1.6 copy-start.1
  170.9 1.6 copy-start

commit v2 on v1

--- a/solution.py
+++ b/solution.py
@@ -229,6 +229,18 @@
         pltpu.make_async_copy(space_out[a], space_out[a], spb_recv.at[a]).wait()
 
 
+def copy_out(*refs):
+    sources, targets, sems = refs[:6], refs[6:12], refs[12]
+    copies = [
+        pltpu.make_async_copy(source, target, sems.at[i])
+        for i, (source, target) in enumerate(zip(sources, targets))
+    ]
+    for copy in copies:
+        copy.start()
+    for copy in copies:
+        copy.wait()
+
+
 def per_device(n_frame, n_patch, *blocks):
     frames, heads, rows, dim = blocks[0].shape
     per_dev = frames * heads // n_patch
@@ -244,13 +256,15 @@
     flat = (frames * heads, rows, dim)
     whole = (frames, heads, rows, dim)
     bf16 = jnp.bfloat16
-    hbm = pl.BlockSpec(memory_space=pl.ANY)
+    hbm = pl.BlockSpec(memory_space=pltpu.HBM)
+    vmem = pl.BlockSpec(memory_space=pltpu.VMEM)
     dma = pltpu.SemaphoreType.DMA
+    sent = [b.reshape(flat) for b in blocks[:4]] + list(blocks[4:])
     outs = pl.pallas_call(
         functools.partial(kernel, plan),
-        out_shape=[jax.ShapeDtypeStruct(flat, bf16)] * 3 + [jax.ShapeDtypeStruct(whole, bf16)] * 3,
+        out_shape=[pltpu.VMEM(flat, bf16)] * 3 + [pltpu.VMEM(whole, bf16)] * 3,
         in_specs=[hbm] * 8,
-        out_specs=[hbm] * 6,
+        out_specs=[vmem] * 6,
         scratch_shapes=[
             pltpu.VMEM((per_dev, 4, length, dim), bf16),
             pltpu.VMEM((per_dev, 3, length, dim), bf16),
@@ -268,10 +282,16 @@
             dma((1,)),
         ],
         compiler_params=pltpu.CompilerParams(
-            collective_id=0, has_side_effects=True, vmem_limit_bytes=56 * 1024 * 1024
+            collective_id=0, has_side_effects=True, vmem_limit_bytes=40 * 1024 * 1024
         ),
-    )(*[b.reshape(flat) for b in blocks[:4]], *blocks[4:])
-    return tuple(o.reshape(whole) for o in outs)
+    )(*[pltpu.with_memory_space_constraint(b, pltpu.HBM) for b in sent])
+    return pl.pallas_call(
+        copy_out,
+        out_shape=[jax.ShapeDtypeStruct(whole, bf16)] * 6,
+        in_specs=[vmem] * 6,
+        out_specs=[hbm] * 6,
+        scratch_shapes=[dma((6,))],
+    )(*[o.reshape(whole) for o in outs])
 
 
 def solution(mesh):

time: 174 us -> 175 us (level)
  Pallas kernels: 163 us -> 169 us
  local copies, waits for them, and re-layouts: 9.73 us -> 5.96 us
    pallas_call x1 -> x2, Pallas kernels: 163 us -> 169 us  [the longest x1 163 us: per_device(): pl.pallas_call(functools.partial(kernel, plan), out_shape=[pltpu.VMEM(fla...]
    unnamed x16 -> x12, local copies, waits for them, and re-layouts: 9.73 us -> 5.96 us
where the time goes in v2:
time: 175 us
  Pallas kernels  169 us (97%)
  local copies, waits for them, and re-layouts  5.96 us (3%)
    pallas_call x1, Pallas kernels, per_device(): pl.pallas_call(functools.partial(kernel, plan), out_shape=[pltpu.VMEM(fla...  163 us
    unnamed x12, local copies, waits for them, and re-layouts  5.96 us
    pallas_call x1, Pallas kernels, per_device(): pl.pallas_call(copy_out, out_shape=[jax.ShapeDtypeStruct(whole, bf16)] *...  5.52 us

profile of v2, /device:TPU:0, one launch (start us, length us, event | category | flops | bytes accessed | tf_op | source)
XLA Modules:
  0.0 175.2 jit_solution(4881235539230687843)
XLA Ops:
  0.6 163.0 %shard_map.127 = (bf16[64,64,128]{2,1,0:T(8,128)(2,1)S(1)}, bf16[64,64,128]{2,1,0:T(8,128)(2,1)S(1)}, bf16[64,64,128]{2,1,0:T(8,128)(2,1)S(1)}, bf16[8,8,64,128]...) custom-call(bf16[64,64,128]{2,1,0:T(8,128)(2,1)} %bitcast.10, ...), custom_call_target="tpu_custom_call" | custom-call | tf_op jit(solution)/shard_map/pallas_call | solution.py:263
  163.7 0.0 copy-start
  163.7 1.0 copy-done
  164.6 0.0 copy-start.1
  164.6 1.0 copy-done.1
  165.7 0.0 copy-start.2
  165.7 1.0 copy-done.2
  166.7 0.0 copy-start.3
  166.7 1.0 copy-done.3
  167.7 0.0 copy-start.4
  167.7 1.0 copy-done.4
  168.6 0.0 copy-start.5
  168.6 1.0 copy-done.5
  169.6 5.5 %shard_map.128 = (bf16[8,8,64,128]{3,2,1,0:T(8,128)(2,1)}, bf16[8,8,64,128]{3,2,1,0:T(8,128)(2,1)}, bf16[8,8,64,128]{3,2,1,0:T(8,128)(2,1)}, bf16[8,8,64,128]{3,...) custom-call(bf16[8,8,64,128]{3,2,1,0:T(8,128)(2,1)} %bitcast.7, ...), custom_call_target="tpu_custom_call" | custom-call | tf_op jit(solution)/shard_map/pallas_call | solution.py:288
Async XLA Ops:
  163.7 1.0 copy-start
  164.6 1.0 copy-start.1
  165.7 1.0 copy-start.2
  166.7 1.0 copy-start.3
  167.7 1.0 copy-start.4
  168.6 1.0 copy-start.5

commit v3 on v2

v3 whole, which is shorter than its diff:
```python
import functools
import math

import jax
import jax.numpy as jnp
from jax import lax
from jax.experimental import pallas as pl
from jax.experimental.pallas import tpu as pltpu
from jax.sharding import PartitionSpec as P

MESH = pl.DeviceIdType.MESH
ROWS = 16
BLOCK = 256


def flip_dot(left, right):
    return lax.dot_general(
        left, right, (((1,), (1,)), ((), ())), preferred_element_type=jnp.float32
    )


def lead_dot(left, right):
    return lax.dot_general(
        left, right, (((0,), (0,)), ((), ())), preferred_element_type=jnp.float32
    )


def attend(length, scale, group, load, store, dk_acc, dv_acc):
    for start in range(0, length, BLOCK):
        rows = min(BLOCK, length - start)
        seen = start + rows if group else length
        query = load(0, start, rows)
        keys = load(1, 0, seen)
        values = load(2, 0, seen)
        upstream = load(3, start, rows)
        scores = flip_dot(keys, query) * scale
        if group:
            gap = (
                lax.broadcasted_iota(jnp.int32, (seen, rows), 1)
                + start
                - lax.broadcasted_iota(jnp.int32, (seen, rows), 0)
            )
            allowed = jnp.logical_and(gap >= 0, (gap & (group - 1)) == 0)
            scores = jnp.where(allowed, scores, -1e30)
        raised = jnp.exp(scores - jnp.max(scores, axis=0, keepdims=True))
        soft = raised * (1.0 / jnp.sum(raised, axis=0, keepdims=True))
        weights = soft.astype(jnp.bfloat16)
        grad_prob = flip_dot(values, upstream)
        delta = jnp.sum(weights.astype(jnp.float32) * grad_prob, axis=0, keepdims=True)
        grad_score = (soft * (grad_prob - delta)).astype(jnp.bfloat16)
        dv = jnp.dot(weights, upstream, preferred_element_type=jnp.float32)
        dk = jnp.dot(grad_score, query, preferred_element_type=jnp.float32)
        store(0, start, (lead_dot(grad_score, keys) * scale).astype(jnp.bfloat16))
        if start == 0 and seen < length:
            dk_acc[pl.ds(seen, length - seen), :] = jnp.zeros((length - seen, dk.shape[1]), jnp.float32)
            dv_acc[pl.ds(seen, length - seen), :] = jnp.zeros((length - seen, dv.shape[1]), jnp.float32)
        if start == 0:
            dk_acc[pl.ds(0, seen), :] = dk
            dv_acc[pl.ds(0, seen), :] = dv
        else:
            dk_acc[pl.ds(0, seen), :] += dk
            dv_acc[pl.ds(0, seen), :] += dv
    store(1, 0, (dk_acc[pl.ds(0, length), :] * scale).astype(jnp.bfloat16))
    store(2, 0, dv_acc[pl.ds(0, length), :].astype(jnp.bfloat16))


def half_scores(part_keys, part_values, query, upstream, scale):
    scores = flip_dot(part_keys, query) * scale
    top = jnp.max(scores, axis=0, keepdims=True)
    raised = jnp.exp(scores - top)
    grad_prob = flip_dot(part_values, upstream)
    mass = jnp.sum(raised, axis=0, keepdims=True)
    drift = jnp.sum(raised * grad_prob, axis=0, keepdims=True)
    return raised, grad_prob, top, mass, drift


def kernel(plan, *refs):
    space_in, time_in = refs[0:4], refs[4:8]
    space_out, time_out = refs[8:11], refs[11:14]
    sp, xp, res, dq_out, dq_in, dq_own, st_out, st_in, e_ring, p_ring = refs[14:24]
    tm, tm_res, dk_acc, dv_acc = refs[24:28]
    (sp_recv, sp_send, xp_recv, xp_send, st_recv, st_send, dq_recv, dq_send) = refs[28:36]
    (res_recv, res_send, tm_recv, tm_send, tmb_recv, tmb_send) = refs[36:]
    n_patch, n_frame, n_seq, rows, frames, heads_dev, span, lag, scale = plan
    half_devs, n_proc = n_patch // 2, n_patch // 4
    per_proc = n_seq // n_proc
    half_rows = half_devs * rows
    ring = lag + 1
    me_p = lax.axis_index("patch")
    me_f = lax.axis_index("frame")
    half = me_p // half_devs
    slot = me_p - half * half_devs
    first_proc = half_devs - n_proc + half * n_proc
    partner = me_p + n_proc - 2 * n_proc * half
    is_proc = jnp.logical_and(me_p >= half_devs - n_proc, me_p < half_devs + n_proc)

    def frame_peer(step):
        return lax.rem(me_f + step, n_frame)

    def time_slot(owner):
        if span == rows:
            return pl.ds(owner * heads_dev, heads_dev), pl.ds(0, span)
        cuts = rows // span
        return (
            pl.ds(owner // cuts, 1),
            pl.ds(pl.multiple_of(lax.rem(owner, cuts) * span, span), span),
        )

    def send(src, dst, send_sem, recv_sem, where):
        pltpu.make_async_remote_copy(
            src_ref=src,
            dst_ref=dst,
            send_sem=send_sem,
            recv_sem=recv_sem,
            device_id=where,
            device_id_type=MESH,
        ).start()

    def wait_bytes(ref, sem):
        pltpu.make_async_copy(ref, ref, sem).wait()

    barrier = pltpu.get_barrier_semaphore()
    for step in range(1, n_patch):
        peer = lax.rem(me_p + step, n_patch)
        pl.semaphore_signal(barrier, inc=1, device_id={"patch": peer}, device_id_type=MESH)
    for step in range(1, n_frame):
        pl.semaphore_signal(barrier, inc=1, device_id={"frame": frame_peer(step)}, device_id_type=MESH)
    pl.semaphore_wait(barrier, n_patch + n_frame - 2)

    my_rows = pl.ds(pl.multiple_of(slot * rows, rows), rows)
    place = (0, 2, 3, 1)

    def send_space(c):
        for j in range(n_proc):
            proc = first_proc + j
            for a in range(4):
                source = space_in[a].at[j * per_proc + c]
                target = sp.at[c, place[a], my_rows]

                @pl.when(proc != me_p)
                def _():
                    send(source, target, sp_send.at[a], sp_recv.at[c], {"patch": proc})

                @pl.when(proc == me_p)
                def _():
                    pltpu.make_async_copy(source, target, sp_recv.at[c]).start()

    def send_time(c):
        here = pl.ds(c, 1)
        there = pl.ds(me_f * frames + c, 1)
        for step in range(1, n_frame):
            peer = frame_peer(step)
            hs, ps = time_slot(peer)
            for a in range(4):
                send(
                    time_in[a].at[here, hs, ps], tm.at[a, there], tm_send.at[0], tm_recv.at[0], {"frame": peer}
                )
        hs, ps = time_slot(me_f)
        for a in range(4):
            pltpu.make_async_copy(time_in[a].at[here, hs, ps], tm.at[a, there], tm_recv.at[0]).start()

    @pl.loop(0, frames)
    def _(c):
        send_space(c)
        send_time(c)

    @pl.loop(frames, per_proc)
    def _(c):
        send_space(c)

    units = span // ROWS
    total = n_frame * frames
    time_units = heads_dev * units

    def time_unit(u):
        hh = u // units
        ps = pl.ds(pl.multiple_of(lax.rem(u, units) * ROWS, ROWS), ROWS)

        def load(a, start, count):
            block = tm[a, pl.ds(start // ROWS, count // ROWS), hh, ps, :]
            return block.reshape(count, block.shape[-1])

        def store(a, start, value):
            count = value.shape[0]
            tm_res[a, pl.ds(start // ROWS, count // ROWS), hh, ps, :] = value.reshape(
                count // ROWS, ROWS, value.shape[1]
            )

        attend(total * ROWS, scale, ROWS, load, store, dk_acc, dv_acc)

    def return_time():
        hs, ps = time_slot(me_f)
        for step in range(1, n_frame):
            peer = frame_peer(step)
            for a in range(3):
                send(
                    tm_res.at[a, pl.ds(peer * frames, frames)],
                    time_out[a].at[:, hs, ps],
                    tmb_send.at[0],
                    tmb_recv.at[a],
                    {"frame": peer},
                )
        for a in range(3):
            pltpu.make_async_copy(
                tm_res.at[a, pl.ds(me_f * frames, frames)], time_out[a].at[:, hs, ps], tmb_recv.at[a]
            ).start()

    def relay(k):
        wait_bytes(sp.at[k], sp_recv.at[k])
        send(sp.at[k, pl.ds(0, 2)], xp.at[k], xp_send.at[0], xp_recv.at[k], {"patch": partner})

    def sides(k):
        return ((sp[k, 0], sp[k, 1]), (xp[k, 0], xp[k, 1]))

    def first_pass(k):
        wait_bytes(xp.at[k], xp_recv.at[k])
        at = lax.rem(k, ring)
        for side, (query, upstream) in enumerate(sides(k)):
            raised, grad_prob, top, mass, drift = half_scores(sp[k, 2], sp[k, 3], query, upstream, scale)
            e_ring[at, side] = raised
            p_ring[at, side] = grad_prob
            st_out[k, side] = jnp.broadcast_to(top, (8, half_rows))
            st_out[k, side, pl.ds(1, 1), :] = mass
            st_out[k, side, pl.ds(2, 1), :] = drift
        send(st_out.at[k], st_in.at[k], st_send.at[0], st_recv.at[k], {"patch": partner})

    def give(k, a):
        seq = (me_p - first_proc) * per_proc + k
        for step in range(1, half_devs):
            other = lax.rem(slot + step, half_devs)
            send(
                res.at[k, a, pl.ds(pl.multiple_of(other * rows, rows), rows)],
                space_out[a].at[seq],
                res_send.at[a],
                res_recv.at[a],
                {"patch": half * half_devs + other},
            )
        pltpu.make_async_copy(res.at[k, a, my_rows], space_out[a].at[seq], res_recv.at[a]).start()

    def second_pass(k):
        wait_bytes(st_in.at[k], st_recv.at[k])
        at = lax.rem(k, ring)
        keys = sp[k, 2]
        dk = dv = None
        for side, (query, upstream) in enumerate(sides(k)):
            mine, theirs = st_out[k, side], st_in[k, 1 - side]
            top = jnp.maximum(mine[0:1], theirs[0:1])
            my_part, their_part = jnp.exp(mine[0:1] - top), jnp.exp(theirs[0:1] - top)
            inverse = 1.0 / (mine[1:2] * my_part + theirs[1:2] * their_part)
            delta = (mine[2:3] * my_part + theirs[2:3] * their_part) * inverse
            soft = e_ring[at, side] * (my_part * inverse)
            weights = soft.astype(jnp.bfloat16)
            grad_score = (soft * (p_ring[at, side] - delta)).astype(jnp.bfloat16)
            dv_side = jnp.dot(weights, upstream, preferred_element_type=jnp.float32)
            dk_side = jnp.dot(grad_score, query, preferred_element_type=jnp.float32)
            dk = dk_side if dk is None else dk + dk_side
            dv = dv_side if dv is None else dv + dv_side
            dq = lead_dot(grad_score, keys) * scale
            if side == 0:
                dq_own[at] = dq
            else:
                dq_out[k] = dq.astype(jnp.bfloat16)
        send(dq_out.at[k], dq_in.at[k], dq_send.at[0], dq_recv.at[k], {"patch": partner})
        res[k, 1] = (dk * scale).astype(jnp.bfloat16)
        res[k, 2] = dv.astype(jnp.bfloat16)
        give(k, 1)
        give(k, 2)

    def finish(k):
        wait_bytes(dq_in.at[k], dq_recv.at[k])
        res[k, 0] = (dq_own[lax.rem(k, ring)] + dq_in[k].astype(jnp.float32)).astype(jnp.bfloat16)
        give(k, 0)

    time_start = per_proc // 2

    @pl.loop(0, per_proc + 3 * lag)
    def _(t):
        for stage, work in enumerate((relay, first_pass, second_pass, finish)):
            k = t - stage * lag

            @pl.when(jnp.logical_and(is_proc, jnp.logical_and(k >= 0, k < per_proc)))
            def _():
                work(k)

        @pl.when(t == time_start)
        def _():
            wait_bytes(tm, tm_recv.at[0])

        @pl.when(jnp.logical_and(t >= time_start, t < time_start + time_units))
        def _():
            time_unit(t - time_start)

        @pl.when(t == time_start + time_units)
        def _():
            return_time()

    @pl.when(is_proc)
    def _():
        for a in range(4):
            if n_seq > per_proc:
                wait_bytes(space_in[a].at[pl.ds(0, n_seq - per_proc)], sp_send.at[a])
        wait_bytes(xp, xp_send.at[0])
        wait_bytes(st_in, st_send.at[0])
        wait_bytes(dq_in, dq_send.at[0])
        for a in range(3):
            wait_bytes(res.at[:, a, pl.ds(0, half_rows - rows)], res_send.at[a])

    @pl.when(jnp.logical_not(is_proc))
    def _():
        for a in range(4):
            wait_bytes(space_in[a], sp_send.at[a])

    away = pl.ds(0, (n_frame - 1) * frames)
    wait_bytes(tm.at[:, away], tm_send.at[0])
    wait_bytes(tm_res.at[:, away], tmb_send.at[0])
    for a in range(3):
        wait_bytes(time_out[a], tmb_recv.at[a])
        wait_bytes(space_out[a], res_recv.at[a])


def copy_out(*refs):
    sources, targets, sems = refs[:6], refs[6:12], refs[12]
    copies = [
        pltpu.make_async_copy(source, target, sems.at[i])
        for i, (source, target) in enumerate(zip(sources, targets))
    ]
    for copy in copies:
        copy.start()
    for copy in copies:
        copy.wait()


def per_device(n_frame, n_patch, *blocks):
    frames, heads, rows, dim = blocks[0].shape
    n_seq = frames * heads
    per_proc = n_seq // (n_patch // 4)
    half_rows = n_patch // 2 * rows
    lag = 3 if half_rows <= 256 else 1
    if n_frame <= heads:
        heads_dev, span = heads // n_frame, rows
    else:
        heads_dev, span = 1, rows * heads // n_frame
    total = n_frame * frames
    scale = 1.0 / math.sqrt(dim)
    plan = (n_patch, n_frame, n_seq, rows, frames, heads_dev, span, lag, scale)
    longest = total * ROWS
    f32 = jnp.float32
    flat = (frames * heads, rows, dim)
    whole = (frames, heads, rows, dim)
    bf16 = jnp.bfloat16
    hbm = pl.BlockSpec(memory_space=pltpu.HBM)
    vmem = pl.BlockSpec(memory_space=pltpu.VMEM)
    dma = pltpu.SemaphoreType.DMA
    sent = [b.reshape(flat) for b in blocks[:4]] + list(blocks[4:])
    outs = pl.pallas_call(
        functools.partial(kernel, plan),
        out_shape=[pltpu.VMEM(flat, bf16)] * 3 + [pltpu.VMEM(whole, bf16)] * 3,
        in_specs=[hbm] * 8,
        out_specs=[vmem] * 6,
        scratch_shapes=[
            pltpu.VMEM((per_proc, 4, half_rows, dim), bf16),
            pltpu.VMEM((per_proc, 2, half_rows, dim), bf16),
            pltpu.VMEM((per_proc, 3, half_rows, dim), bf16),
            pltpu.VMEM((per_proc, half_rows, dim), bf16),
            pltpu.VMEM((per_proc, half_rows, dim), bf16),
            pltpu.VMEM((lag + 1, half_rows, dim), f32),
            pltpu.VMEM((per_proc, 2, 8, half_rows), f32),
            pltpu.VMEM((per_proc, 2, 8, half_rows), f32),
            pltpu.VMEM((lag + 1, 2, half_rows, half_rows), f32),
            pltpu.VMEM((lag + 1, 2, half_rows, half_rows), f32),
            pltpu.VMEM((4, total, heads_dev, span, dim), bf16),
            pltpu.VMEM((3, total, heads_dev, span, dim), bf16),
            pltpu.VMEM((longest, dim), f32),
            pltpu.VMEM((longest, dim), f32),
            dma((per_proc,)),
            dma((4,)),
            dma((per_proc,)),
            dma((1,)),
            dma((per_proc,)),
            dma((1,)),
            dma((per_proc,)),
            dma((1,)),
            dma((3,)),
            dma((3,)),
            dma((1,)),
            dma((1,)),
            dma((3,)),
            dma((1,)),
        ],
        compiler_params=pltpu.CompilerParams(
            collective_id=0, has_side_effects=True, vmem_limit_bytes=52 * 1024 * 1024
        ),
    )(*[pltpu.with_memory_space_constraint(b, pltpu.HBM) for b in sent])
    return pl.pallas_call(
        copy_out,
        out_shape=[jax.ShapeDtypeStruct(whole, bf16)] * 6,
        in_specs=[vmem] * 6,
        out_specs=[hbm] * 6,
        scratch_shapes=[dma((6,))],
        compiler_params=pltpu.CompilerParams(vmem_limit_bytes=1024 * 1024),
    )(*[o.reshape(whole) for o in outs])


def solution(mesh):
    spec = P("frame", None, "patch", None)
    return jax.shard_map(
        functools.partial(per_device, mesh.shape["frame"], mesh.shape["patch"]),
        mesh=mesh,
        in_specs=(spec,) * 8,
        out_specs=(spec,) * 6,
        check_vma=False,
    )
```

time: 175 us -> 167 us (0.954)
  local copies, waits for them, and re-layouts: 5.96 us -> 0 us
  Pallas kernels: 169 us -> 166 us
    unnamed x12 -> x0, local copies, waits for them, and re-layouts: 5.96 us -> none
    pallas_call x1, Pallas kernels: 5.52 us -> 2.72 us  [per_device(): pl.pallas_call(copy_out, out_shape=[jax.ShapeDtypeStruct(whole, bf16)] *...]
where the time goes in v3:
time: 167 us
  Pallas kernels  166 us (99%)
    pallas_call x1, Pallas kernels, per_device(): pl.pallas_call(functools.partial(kernel, plan), out_shape=[pltpu.VMEM(fla...  163 us

profile of v3, /device:TPU:0, one launch (start us, length us, event | category | flops | bytes accessed | tf_op | source)
XLA Modules:
  0.0 166.6 jit_solution(9698510827416392817)
XLA Ops:
  0.6 163.3 %shard_map.127 = (bf16[64,64,128]{2,1,0:T(8,128)(2,1)S(1)}, bf16[64,64,128]{2,1,0:T(8,128)(2,1)S(1)}, bf16[64,64,128]{2,1,0:T(8,128)(2,1)S(1)}, bf16[8,8,64,128]...) custom-call(bf16[64,64,128]{2,1,0:T(8,128)(2,1)} %bitcast.10, ...), custom_call_target="tpu_custom_call" | custom-call | tf_op jit(solution)/shard_map/pallas_call | solution.py:355
  163.9 2.7 %shard_map.128 = (bf16[8,8,64,128]{3,2,1,0:T(8,128)(2,1)}, bf16[8,8,64,128]{3,2,1,0:T(8,128)(2,1)}, bf16[8,8,64,128]{3,2,1,0:T(8,128)(2,1)}, bf16[8,8,64,128]{3,...) custom-call(bf16[8,8,64,128]{3,2,1,0:T(8,128)(2,1)S(1)} %bitcast.7, ...), custom_call_target="tpu_custom_call" | custom-call | tf_op jit(solution)/shard_map/pallas_call | solution.py:394

commit v4 on v3

--- a/solution.py
+++ b/solution.py
@@ -159,14 +159,26 @@
         for a in range(4):
             pltpu.make_async_copy(time_in[a].at[here, hs, ps], tm.at[a, there], tm_recv.at[0]).start()
 
-    @pl.loop(0, frames)
-    def _(c):
-        send_space(c)
-        send_time(c)
-
-    @pl.loop(frames, per_proc)
-    def _(c):
-        send_space(c)
+    ahead = min(6, per_proc)
+    stride = max(1, per_proc // (2 * frames))
+
+    def paced_time(c):
+        @pl.when(jnp.logical_and(lax.rem(c, stride) == 0, c < frames * stride))
+        def _():
+            send_time(c // stride)
+
+    @pl.when(is_proc)
+    def _():
+        @pl.loop(0, ahead)
+        def _(c):
+            send_space(c)
+
+    @pl.when(jnp.logical_not(is_proc))
+    def _():
+        @pl.loop(0, per_proc)
+        def _(c):
+            send_space(c)
+            paced_time(c)
 
     units = span // ROWS
     total = n_frame * frames
@@ -188,13 +200,17 @@
 
         attend(total * ROWS, scale, ROWS, load, store, dk_acc, dv_acc)
 
-    def return_time():
-        hs, ps = time_slot(me_f)
+    def return_time(hh):
+        if span == rows:
+            hs, ps = pl.ds(me_f * heads_dev + hh, 1), pl.ds(0, span)
+        else:
+            hs, ps = time_slot(me_f)
+        head = pl.ds(hh, 1)
         for step in range(1, n_frame):
             peer = frame_peer(step)
             for a in range(3):
                 send(
-                    tm_res.at[a, pl.ds(peer * frames, frames)],
+                    tm_res.at[a, pl.ds(peer * frames, frames), head],
                     time_out[a].at[:, hs, ps],
                     tmb_send.at[0],
                     tmb_recv.at[a],
@@ -202,7 +218,7 @@
                 )
         for a in range(3):
             pltpu.make_async_copy(
-                tm_res.at[a, pl.ds(me_f * frames, frames)], time_out[a].at[:, hs, ps], tmb_recv.at[a]
+                tm_res.at[a, pl.ds(me_f * frames, frames), head], time_out[a].at[:, hs, ps], tmb_recv.at[a]
             ).start()
 
     def relay(k):
@@ -271,7 +287,7 @@
         res[k, 0] = (dq_own[lax.rem(k, ring)] + dq_in[k].astype(jnp.float32)).astype(jnp.bfloat16)
         give(k, 0)
 
-    time_start = per_proc // 2
+    time_start = per_proc // 2 + 2
 
     @pl.loop(0, per_proc + 3 * lag)
     def _(t):
@@ -282,17 +298,28 @@
             def _():
                 work(k)
 
+            if stage == 0:
+
+                @pl.when(jnp.logical_and(is_proc, t < per_proc - ahead))
+                def _():
+                    send_space(t + ahead)
+
+                @pl.when(is_proc)
+                def _():
+                    paced_time(t)
+
         @pl.when(t == time_start)
         def _():
             wait_bytes(tm, tm_recv.at[0])
 
         @pl.when(jnp.logical_and(t >= time_start, t < time_start + time_units))
         def _():
-            time_unit(t - time_start)
-
-        @pl.when(t == time_start + time_units)
-        def _():
-            return_time()
+            u = t - time_start
+            time_unit(u)
+
+            @pl.when(lax.rem(u, units) == units - 1)
+            def _():
+                return_time(u // units)
 
     @pl.when(is_proc)
     def _():

time: 167 us -> 167 us (level)
  no operation moved by 1% of the time
where the time goes in v4:
time: 167 us
  Pallas kernels  166 us (99%)
    pallas_call x1, Pallas kernels, per_device(): pl.pallas_call(functools.partial(kernel, plan), out_shape=[pltpu.VMEM(fla...  163 us

profile of v4, /device:TPU:0, one launch (start us, length us, event | category | flops | bytes accessed | tf_op | source)
XLA Modules:
  0.0 166.6 jit_solution(8204525742620943884)
XLA Ops:
  0.6 163.3 %shard_map.127 = (bf16[64,64,128]{2,1,0:T(8,128)(2,1)S(1)}, bf16[64,64,128]{2,1,0:T(8,128)(2,1)S(1)}, bf16[64,64,128]{2,1,0:T(8,128)(2,1)S(1)}, bf16[8,8,64,128]...) custom-call(bf16[64,64,128]{2,1,0:T(8,128)(2,1)} %bitcast.10, ...), custom_call_target="tpu_custom_call" | custom-call | tf_op jit(solution)/shard_map/pallas_call | solution.py:382
  163.9 2.7 %shard_map.128 = (bf16[8,8,64,128]{3,2,1,0:T(8,128)(2,1)}, bf16[8,8,64,128]{3,2,1,0:T(8,128)(2,1)}, bf16[8,8,64,128]{3,2,1,0:T(8,128)(2,1)}, bf16[8,8,64,128]{3,...) custom-call(bf16[8,8,64,128]{3,2,1,0:T(8,128)(2,1)S(1)} %bitcast.7, ...), custom_call_target="tpu_custom_call" | custom-call | tf_op jit(solution)/shard_map/pallas_call | solution.py:421

commit v5 on v4

--- a/solution.py
+++ b/solution.py
@@ -83,16 +83,20 @@
     (res_recv, res_send, tm_recv, tm_send, tmb_recv, tmb_send) = refs[36:]
     n_patch, n_frame, n_seq, rows, frames, heads_dev, span, lag, scale = plan
     half_devs, n_proc = n_patch // 2, n_patch // 4
-    per_proc = n_seq // n_proc
+    n_out = n_seq // n_proc // 4
+    n_mid = n_seq // n_proc - n_out
+    ratio = n_mid // n_out
     half_rows = half_devs * rows
     ring = lag + 1
     me_p = lax.axis_index("patch")
     me_f = lax.axis_index("frame")
     half = me_p // half_devs
     slot = me_p - half * half_devs
-    first_proc = half_devs - n_proc + half * n_proc
-    partner = me_p + n_proc - 2 * n_proc * half
-    is_proc = jnp.logical_and(me_p >= half_devs - n_proc, me_p < half_devs + n_proc)
+    mid_slot, out_slot = n_proc * (1 - half), n_proc * half
+    is_mid = slot // n_proc == 1 - half
+    lane = lax.rem(slot, n_proc)
+    first_seq = jnp.where(is_mid, lane * n_mid, n_proc * n_mid + lane * n_out)
+    partner = (1 - half) * half_devs + lax.rem(slot + n_proc, half_devs)
 
     def frame_peer(step):
         return lax.rem(me_f + step, n_frame)
@@ -130,20 +134,27 @@
     my_rows = pl.ds(pl.multiple_of(slot * rows, rows), rows)
     place = (0, 2, 3, 1)
 
+    def send_rows(owner, seq, c):
+        for a in range(4):
+            source = space_in[a].at[seq]
+            target = sp.at[c, place[a], my_rows]
+
+            @pl.when(owner != slot)
+            def _():
+                send(source, target, sp_send.at[a], sp_recv.at[c], {"patch": half * half_devs + owner})
+
+            @pl.when(owner == slot)
+            def _():
+                pltpu.make_async_copy(source, target, sp_recv.at[c]).start()
+
     def send_space(c):
         for j in range(n_proc):
-            proc = first_proc + j
-            for a in range(4):
-                source = space_in[a].at[j * per_proc + c]
-                target = sp.at[c, place[a], my_rows]
-
-                @pl.when(proc != me_p)
-                def _():
-                    send(source, target, sp_send.at[a], sp_recv.at[c], {"patch": proc})
-
-                @pl.when(proc == me_p)
-                def _():
-                    pltpu.make_async_copy(source, target, sp_recv.at[c]).start()
+            send_rows(mid_slot + j, j * n_mid + c, c)
+
+        @pl.when(lax.rem(c, ratio) == 0)
+        def _():
+            for j in range(n_proc):
+                send_rows(out_slot + j, n_proc * n_mid + j * n_out + c // ratio, c // ratio)
 
     def send_time(c):
         here = pl.ds(c, 1)
@@ -159,26 +170,11 @@
         for a in range(4):
             pltpu.make_async_copy(time_in[a].at[here, hs, ps], tm.at[a, there], tm_recv.at[0]).start()
 
-    ahead = min(6, per_proc)
-    stride = max(1, per_proc // (2 * frames))
-
-    def paced_time(c):
-        @pl.when(jnp.logical_and(lax.rem(c, stride) == 0, c < frames * stride))
-        def _():
-            send_time(c // stride)
-
-    @pl.when(is_proc)
-    def _():
-        @pl.loop(0, ahead)
-        def _(c):
-            send_space(c)
-
-    @pl.when(jnp.logical_not(is_proc))
-    def _():
-        @pl.loop(0, per_proc)
-        def _(c):
-            send_space(c)
-            paced_time(c)
+    ahead = min(6, n_mid)
+
+    @pl.loop(0, ahead)
+    def _(c):
+        send_space(c)
 
     units = span // ROWS
     total = n_frame * frames
@@ -241,7 +237,7 @@
         send(st_out.at[k], st_in.at[k], st_send.at[0], st_recv.at[k], {"patch": partner})
 
     def give(k, a):
-        seq = (me_p - first_proc) * per_proc + k
+        seq = first_seq + k
         for step in range(1, half_devs):
             other = lax.rem(slot + step, half_devs)
             send(
@@ -287,55 +283,70 @@
         res[k, 0] = (dq_own[lax.rem(k, ring)] + dq_in[k].astype(jnp.float32)).astype(jnp.bfloat16)
         give(k, 0)
 
-    time_start = per_proc // 2 + 2
-
-    @pl.loop(0, per_proc + 3 * lag)
+    time_start = frames
+    pace = 2
+    steps = max(n_mid + 3 * lag, (n_out + 3) * ratio, time_start + pace * time_units)
+
+    @pl.loop(0, steps)
     def _(t):
         for stage, work in enumerate((relay, first_pass, second_pass, finish)):
-            k = t - stage * lag
-
-            @pl.when(jnp.logical_and(is_proc, jnp.logical_and(k >= 0, k < per_proc)))
+            k_mid = t - stage * lag
+            k_out = t // ratio - stage
+            go_mid = jnp.logical_and(is_mid, jnp.logical_and(k_mid >= 0, k_mid < n_mid))
+            go_out = jnp.logical_and(
+                jnp.logical_and(jnp.logical_not(is_mid), lax.rem(t, ratio) == 0),
+                jnp.logical_and(k_out >= 0, k_out < n_out),
+            )
+
+            @pl.when(jnp.logical_or(go_mid, go_out))
             def _():
-                work(k)
+                work(jnp.where(is_mid, k_mid, k_out))
 
             if stage == 0:
 
-                @pl.when(jnp.logical_and(is_proc, t < per_proc - ahead))
+                @pl.when(t < n_mid - ahead)
                 def _():
                     send_space(t + ahead)
 
-                @pl.when(is_proc)
+                @pl.when(t < frames)
                 def _():
-                    paced_time(t)
+                    send_time(t)
 
         @pl.when(t == time_start)
         def _():
             wait_bytes(tm, tm_recv.at[0])
 
-        @pl.when(jnp.logical_and(t >= time_start, t < time_start + time_units))
+        u = (t - time_start) // pace
+
+        @pl.when(
+            jnp.logical_and(
+                jnp.logical_and(t >= time_start, lax.rem(t, pace) == time_start % pace), u < time_units
+            )
+        )
         def _():
-            u = t - time_start
             time_unit(u)
 
             @pl.when(lax.rem(u, units) == units - 1)
             def _():
                 return_time(u // units)
 
-    @pl.when(is_proc)
+    def settle(count):
+        part = pl.ds(0, count)
+        for a in range(4):
+            wait_bytes(space_in[a].at[pl.ds(0, n_seq - count)], sp_send.at[a])
+        wait_bytes(xp.at[part], xp_send.at[0])
+        wait_bytes(st_in.at[part], st_send.at[0])
+        wait_bytes(dq_in.at[part], dq_send.at[0])
+        for a in range(3):
+            wait_bytes(res.at[part, a, pl.ds(0, half_rows - rows)], res_send.at[a])
+
+    @pl.when(is_mid)
     def _():
-        for a in range(4):
-            if n_seq > per_proc:
-                wait_bytes(space_in[a].at[pl.ds(0, n_seq - per_proc)], sp_send.at[a])
-        wait_bytes(xp, xp_send.at[0])
-        wait_bytes(st_in, st_send.at[0])
-        wait_bytes(dq_in, dq_send.at[0])
-        for a in range(3):
-            wait_bytes(res.at[:, a, pl.ds(0, half_rows - rows)], res_send.at[a])
-
-    @pl.when(jnp.logical_not(is_proc))
+        settle(n_mid)
+
+    @pl.when(jnp.logical_not(is_mid))
     def _():
-        for a in range(4):
-            wait_bytes(space_in[a], sp_send.at[a])
+        settle(n_out)
 
     away = pl.ds(0, (n_frame - 1) * frames)
     wait_bytes(tm.at[:, away], tm_send.at[0])
@@ -360,7 +371,8 @@
 def per_device(n_frame, n_patch, *blocks):
     frames, heads, rows, dim = blocks[0].shape
     n_seq = frames * heads
-    per_proc = n_seq // (n_patch // 4)
+    n_pair = n_seq // (n_patch // 4)
+    n_mid = n_pair - n_pair // 4
     half_rows = n_patch // 2 * rows
     lag = 3 if half_rows <= 256 else 1
     if n_frame <= heads:
@@ -385,27 +397,27 @@
         in_specs=[hbm] * 8,
         out_specs=[vmem] * 6,
         scratch_shapes=[
-            pltpu.VMEM((per_proc, 4, half_rows, dim), bf16),
-            pltpu.VMEM((per_proc, 2, half_rows, dim), bf16),
-            pltpu.VMEM((per_proc, 3, half_rows, dim), bf16),
-            pltpu.VMEM((per_proc, half_rows, dim), bf16),
-            pltpu.VMEM((per_proc, half_rows, dim), bf16),
+            pltpu.VMEM((n_mid, 4, half_rows, dim), bf16),
+            pltpu.VMEM((n_mid, 2, half_rows, dim), bf16),
+            pltpu.VMEM((n_mid, 3, half_rows, dim), bf16),
+            pltpu.VMEM((n_mid, half_rows, dim), bf16),
+            pltpu.VMEM((n_mid, half_rows, dim), bf16),
             pltpu.VMEM((lag + 1, half_rows, dim), f32),
-            pltpu.VMEM((per_proc, 2, 8, half_rows), f32),
-            pltpu.VMEM((per_proc, 2, 8, half_rows), f32),
+            pltpu.VMEM((n_mid, 2, 8, half_rows), f32),
+            pltpu.VMEM((n_mid, 2, 8, half_rows), f32),
             pltpu.VMEM((lag + 1, 2, half_rows, half_rows), f32),
             pltpu.VMEM((lag + 1, 2, half_rows, half_rows), f32),
             pltpu.VMEM((4, total, heads_dev, span, dim), bf16),
             pltpu.VMEM((3, total, heads_dev, span, dim), bf16),
             pltpu.VMEM((longest, dim), f32),
             pltpu.VMEM((longest, dim), f32),
-            dma((per_proc,)),
+            dma((n_mid,)),
             dma((4,)),
-            dma((per_proc,)),
-            dma((1,)),
-            dma((per_proc,)),
-            dma((1,)),
-            dma((per_proc,)),
+            dma((n_mid,)),
+            dma((1,)),
+            dma((n_mid,)),
+            dma((1,)),
+            dma((n_mid,)),
             dma((1,)),
             dma((3,)),
             dma((3,)),

time: 167 us -> 170 us (1.018)
  Pallas kernels: 166 us -> 169 us
    pallas_call x1, Pallas kernels: 163 us -> 166 us  [per_device(): pl.pallas_call(functools.partial(kernel, plan), out_shape=[pltpu.VMEM(fla...]
where the time goes in v5:
time: 170 us
  Pallas kernels  169 us (99%)
    pallas_call x1, Pallas kernels, per_device(): pl.pallas_call(functools.partial(kernel, plan), out_shape=[pltpu.VMEM(fla...  166 us

profile of v5, /device:TPU:0, one launch (start us, length us, event | category | flops | bytes accessed | tf_op | source)
XLA Modules:
  0.0 169.7 jit_solution(5777289169444986734)
XLA Ops:
  0.6 166.3 %shard_map.127 = (bf16[64,64,128]{2,1,0:T(8,128)(2,1)S(1)}, bf16[64,64,128]{2,1,0:T(8,128)(2,1)S(1)}, bf16[64,64,128]{2,1,0:T(8,128)(2,1)S(1)}, bf16[8,8,64,128]...) custom-call(bf16[64,64,128]{2,1,0:T(8,128)(2,1)} %bitcast.10, ...), custom_call_target="tpu_custom_call" | custom-call | tf_op jit(solution)/shard_map/pallas_call | solution.py:394
  166.9 2.7 %shard_map.128 = (bf16[8,8,64,128]{3,2,1,0:T(8,128)(2,1)}, bf16[8,8,64,128]{3,2,1,0:T(8,128)(2,1)}, bf16[8,8,64,128]{3,2,1,0:T(8,128)(2,1)}, bf16[8,8,64,128]{3,...) custom-call(bf16[8,8,64,128]{3,2,1,0:T(8,128)(2,1)S(1)} %bitcast.7, ...), custom_call_target="tpu_custom_call" | custom-call | tf_op jit(solution)/shard_map/pallas_call | solution.py:433

commit v6 on v2

--- a/solution.py
+++ b/solution.py
@@ -291,6 +291,7 @@
         in_specs=[vmem] * 6,
         out_specs=[hbm] * 6,
         scratch_shapes=[dma((6,))],
+        compiler_params=pltpu.CompilerParams(vmem_limit_bytes=1024 * 1024),
     )(*[o.reshape(whole) for o in outs])
 
 

time: 175 us -> 167 us (0.954)
  local copies, waits for them, and re-layouts: 5.96 us -> 0 us
  Pallas kernels: 169 us -> 166 us
    unnamed x12 -> x0, local copies, waits for them, and re-layouts: 5.96 us -> none
    pallas_call x1, Pallas kernels: 5.52 us -> 2.72 us  [per_device(): pl.pallas_call(copy_out, out_shape=[jax.ShapeDtypeStruct(whole, bf16)] *...]
where the time goes in v6:
time: 167 us; the launch traced here: 166 us
  Pallas kernels  166 us (99%)
    pallas_call x1, Pallas kernels, per_device(): pl.pallas_call(functools.partial(kernel, plan), out_shape=[pltpu.VMEM(fla...  163 us

profile of v6, /device:TPU:0, one launch (start us, length us, event | category | flops | bytes accessed | tf_op | source)
XLA Modules:
  0.0 166.4 jit_solution(17317772787522652016)
XLA Ops:
  0.6 163.0 %shard_map.127 = (bf16[64,64,128]{2,1,0:T(8,128)(2,1)S(1)}, bf16[64,64,128]{2,1,0:T(8,128)(2,1)S(1)}, bf16[64,64,128]{2,1,0:T(8,128)(2,1)S(1)}, bf16[8,8,64,128]...) custom-call(bf16[64,64,128]{2,1,0:T(8,128)(2,1)} %bitcast.10, ...), custom_call_target="tpu_custom_call" | custom-call | tf_op jit(solution)/shard_map/pallas_call | solution.py:263
  163.7 2.7 %shard_map.128 = (bf16[8,8,64,128]{3,2,1,0:T(8,128)(2,1)}, bf16[8,8,64,128]{3,2,1,0:T(8,128)(2,1)}, bf16[8,8,64,128]{3,2,1,0:T(8,128)(2,1)}, bf16[8,8,64,128]{3,...) custom-call(bf16[8,8,64,128]{3,2,1,0:T(8,128)(2,1)S(1)} %bitcast.7, ...), custom_call_target="tpu_custom_call" | custom-call | tf_op jit(solution)/shard_map/pallas_call | solution.py:288
